TPU v7x, 512 devices: a whole 4x8x8 slice. The times are simulated.
512 devices in a mesh: lat: 4 (over x_hi, core), lon: 128 (over z, y, x_lo).
Axes of the slice: x: 4 (x_hi: 2, x_lo: 2; x = x_hi * 2 + x_lo), y: 8, z: 8, core: 2. Of those that a mesh axis runs over, the one named last changes fastest.
Arguments:
- atmosphere: float32 [256, 1024, 256], P('lat', 'lon'), may hold values from -6 to 6
- disc_basis: float32 [3, 256, 5, 5], P(None, 'lat'), may hold values from -1.25 to 1.25
- polar_basis: float32 [2, 3, 2, 4, 1024], replicated, may hold values from -0.09375 to 0.09375
- widths: int32 [256], P('lat'), may hold values from 0 to 2
- weights: float32 [1, 3, 256, 256], P(None, None, 'lat'), may hold values from -0.21875 to 0.21875
- channel_bias: float32 [1, 256], replicated, may hold values from -3 to 3
Outputs:
- forecast: float32 [256, 1024, 256], P('lat', 'lon')
All inputs are finite; a program needn't handle non-finite values.
Results may differ from a plain program's by a relative error of at most 0.0001.
Values sent between devices are 32-bit elements; how exact they have to be, the bound alone decides.
A program may use at most 128 MiB of HBM per device.

v0:
```python
import jax
import jax.numpy as jnp
from jax import lax
from jax.sharding import PartitionSpec as P


def extended(block, sides, width):
    for axis, dim in sides:
        count = lax.axis_size(axis)
        forward = [(i, i + 1) for i in range(count - 1)]
        forward.append((count - 1, 0))
        backward = [(target, source) for source, target in forward]
        low = lax.ppermute(
            lax.slice_in_dim(block, block.shape[dim] - width, None, axis=dim), axis, forward
        )
        high = lax.ppermute(lax.slice_in_dim(block, 0, width, axis=dim), axis, backward)
        block = jnp.concatenate([low, block, high], axis=dim)
    return block


def polar_mix(sources, basis_half, mixing, lon_dev, lon_total):
    local_cols = lax.axis_index("lon") * lon_dev + jnp.arange(lon_dev, dtype=jnp.int32)
    piece = lax.all_gather(sources, "lon", axis=1, tiled=True)
    count = piece.shape[1]
    source_cols = jnp.arange(count, dtype=jnp.int32)
    gaps = (source_cols[None, :] - local_cols[:, None]) % lon_total
    kernel = jnp.take(basis_half, gaps, axis=3)
    polar_taps = jnp.einsum("kpqjn,qnc->kpjc", kernel, piece, precision=lax.Precision.HIGHEST)
    return jnp.einsum("kpjc,kcd->pjd", polar_taps, mixing, precision=lax.Precision.HIGHEST)


def on_device(atmosphere, disc_basis, polar_basis, widths, weights, channel_bias):
    lat_dev, lon_dev, channels = atmosphere.shape
    reach_rows = (disc_basis.shape[2] - 1) // 2
    polar_count = polar_basis.shape[2]
    source_count = polar_basis.shape[3]
    lon_total = lon_dev * lax.axis_size("lon")
    lat_bands = lax.axis_size("lat")
    band_index = lax.axis_index("lat")
    mixing_all = lax.all_gather(weights, "lat", axis=2, tiled=True)
    offsets = jnp.abs(jnp.arange(2 * reach_rows + 1) - reach_rows)
    taps_mask = (offsets[None, :] <= widths[:, None]).astype(jnp.float32)
    row_ids = jnp.arange(lat_dev)
    north_rows = ((band_index == 0) & (row_ids < polar_count))[:, None, None]
    south_rows = ((band_index == lat_bands - 1) & (row_ids >= lat_dev - polar_count))[:, None, None]
    padding = jnp.zeros((lat_dev - polar_count, lon_dev, channels), jnp.float32)
    northern = band_index < lat_bands // 2
    basis_half = jnp.where(northern, polar_basis[0], polar_basis[1])
    state = atmosphere
    mixing = mixing_all[0]
    padded = extended(state, (("lat", 0), ("lon", 1)), reach_rows)
    mixed = jnp.zeros((lat_dev * lon_dev, channels), jnp.float32)
    for basis_index in range(disc_basis.shape[0]):
        summed = jnp.zeros_like(state)
        for row_step in range(2 * reach_rows + 1):
            for col_step in range(2 * reach_rows + 1):
                weight_row = disc_basis[basis_index, :, row_step, col_step] * taps_mask[:, col_step]
                window = padded[row_step : row_step + lat_dev, col_step : col_step + lon_dev]
                summed = summed + weight_row[:, None, None] * window
        mixed = mixed + jnp.dot(
            summed.reshape(-1, channels), mixing[basis_index], precision=lax.Precision.HIGHEST
        )
    mixed = mixed.reshape(lat_dev, lon_dev, channels)
    top_rows = state[:source_count]
    bottom_rows = state[lat_dev - source_count :][::-1]
    sources = jnp.where(northern, top_rows, bottom_rows)
    polar_part = polar_mix(sources, basis_half, mixing, lon_dev, lon_total)
    top_fill = jnp.concatenate([polar_part, padding], axis=0)
    bottom_fill = jnp.concatenate([padding, polar_part[::-1]], axis=0)
    mixed = jnp.where(north_rows, top_fill, jnp.where(south_rows, bottom_fill, mixed))
    state = jax.nn.gelu(mixed + channel_bias[0], approximate=False)
    return state


def solution(mesh):
    return jax.shard_map(
        on_device,
        mesh=mesh,
        in_specs=(
            P("lat", "lon", None),
            P(None, "lat", None, None),
            P(),
            P("lat"),
            P(None, None, "lat", None),
            P(),
        ),
        out_specs=P("lat", "lon", None),
        check_vma=False,
    )
```

profile of v0, /device:TPU:6, one launch (start us, length us, event | category | flops | bytes accessed | tf_op | source)
XLA Modules:
  0.0 627.0 jit_solution(2382764604974488797)
XLA Ops:
  6.5 0.0 all-gather.2.cloned.1.call-start
  6.5 0.8 slice.493
  7.3 1.4 reverse_select_fusion
  8.7 0.0 all-gather.2.cloned.1.call-update
  8.7 1.3 fusion.349
  10.0 1.9 collective-permute-start
  12.0 5.1 collective-permute-start.1
  17.1 1.0 fusion.350
  18.1 0.0 copy-start.3
  18.1 1.7 copy.20
  19.7 0.0 copy-start.7
  19.8 0.0 copy-start.6
  19.8 3.4 copy.21
  23.2 0.0 copy-done.7
  23.2 0.1 compare_convert_fusion
  23.2 0.0 copy-done.6
  23.2 0.6 bitcast_multiply_fusion.49
  23.8 0.6 bitcast_multiply_fusion.74
  24.5 0.6 bitcast_multiply_fusion.73
  25.1 0.6 bitcast_multiply_fusion.22
  25.7 0.6 bitcast_multiply_fusion.1
  26.3 0.6 bitcast_multiply_fusion
  26.9 0.6 bitcast_multiply_fusion.24
  27.5 0.6 bitcast_multiply_fusion.23
  28.1 0.1 fusion.283
  28.2 0.0 copy-done.3
  28.3 9.7 %all_gather.7 = f32[1,3,256,256]{3,2,1,0:T(8,128)} all-gather(f32[1,3,64,256]{3,2,1,0:T(8,128)S(1)} %copy-done.3), channel_id=1, replica_groups=mesh['lat'=4,'lon'=128] {'lat'}, dimensions={2}, use_global_device_ids=true | all-gather | bytes 983040 | tf_op jit(solution)/shard_map/all_gather | solution.py:40
  37.9 5.2 select_bitcast_fusion
  43.1 0.1 compare_and_fusion
  43.2 0.0 collective-permute-done
  43.2 0.7 constant_dynamic-update-slice_fusion.2
  43.9 0.0 copy-done.1
  43.9 0.1 constant_dynamic-update-slice_fusion.1
  44.1 0.0 copy-start.63
  44.1 0.0 collective-permute-done.1
  44.1 0.0 copy-start.4
  44.1 0.1 fusion.348
  44.2 3.7 collective-permute-start.2
  48.0 0.7 copy.25
  48.6 0.0 copy-done.4
  48.6 5.6 collective-permute-start.3
  54.2 0.0 copy-done.63
  54.2 1.3 bitcast_multiply_fusion.72
  55.5 87.6 %gather_fusion = f32[8192,3,2,4]{3,2,1,0:T(2,128)} fusion(f32[3,2,4,1024]{2,1,3,0:T(2,128)} %select_bitcast_fusion, s32[8192]{0:T(1024)S(1)} %bitcast_clamp_fusion), kind=kCustom, calls=%fused_computation | custom fusion | bytes 1605632 | tf_op jit(solution)/shard_map/jit(_take)/gather | solution.py:27
  143.1 0.0 copy-start.36
  143.1 0.0 copy-start.37
  143.1 0.0 copy-start.38
  143.1 0.0 copy-start.55
  143.2 0.0 copy-start.56
  143.2 0.0 copy-start.57
  143.2 0.0 copy-start.58
  143.2 0.0 copy-start.59
  143.2 20.1 %copy.22 = f32[8,1024,3,2,4]{1,0,4,2,3:T(8,128)S(1)} copy(f32[8,1024,3,2,4]{4,3,2,1,0:T(2,128)} %bitcast.288) | data formatting | bytes 1572864 | tf_op jit(solution)/shard_map/jit(_take)/gather | solution.py:27
  163.4 0.6 compare_and_fusion.1
  164.0 0.0 collective-permute-done.2
  164.0 0.1 copy.24
  164.0 0.0 collective-permute-done.3
  164.1 1.0 copy.26
  165.4 4.8 fusion.34
  170.5 5.8 convolution_add_fusion.1
  176.4 431.4 %all-gather.2.cloned.1.call-done = f32[4,1024,256]{2,1,0:T(8,128)} async-done(((f32[4,8,256]{2,1,0:T(8,128)}), f32[4,1024,256]{2,1,0:T(8,128)}) %all-gather.2.cloned.1.call-update) | async-done | bytes 4194320 | tf_op jit(solution)/shard_map/all_gather | solution.py:23
  607.8 4.4 fusion.6
  612.2 0.4 convolution_bitcast_fusion
  612.8 7.4 %fusion.13 = f32[64,8,256]{2,1,0:T(8,128)} fusion(f32[512,256]{1,0:T(8,128)} %convolution_add_fusion.1, f32[64,8,256]{2,1,0:T(8,128)S(1)} %copy-done.2, f32[2,8,256]{2,1,0:T(8,128)S(1)} %rev.7, f32[2,8,256]{2,1,0:T(8,128)S(1)} %convolution_bitcast_fusion, f32[66,8,256]{2,1,0:T(8,128)S(1)} %get-tuple-element.90, f32[66,8,256]{2,1,0:T(8,128)} %copy-done.63, ...), kind=kOutput, calls=%fused_computation.53 | convolution fusion | flops 420610048 | bytes 4815360 | tf_op jit(solution)/shard_map/dot_general | solution.py:60
  (115 shorter events, 0.3 us)
Async XLA Ops:
  6.5 601.3 %all-gather.2.cloned.1.call-start = ((), (), s32[]{:S(2)}) async-start(), calls=%async_computation | async-start | bytes 4227072 | tf_op jit(solution)/shard_map/all_gather | solution.py:23
  10.0 33.2 %collective-permute-start = (f32[2,8,256]{2,1,0:T(8,128)}, f32[2,8,256]{2,1,0:T(8,128)}, u32[]{:S(2)}, u32[]{:S(2)}) collective-permute-start(f32[2,8,256]{2,1,0:T(8,128)} %get-tuple-element.10), channel_id=1, source_target_pairs={{0,128},{128,256},{256,384},{384,0},{1,129},{129,257},{257,385},{3... | collective-permute-start | bytes 49160 | tf_op jit(solution)/shard_map/ppermute | solution.py:13
  12.0 32.1 %collective-permute-start.1 = (f32[2,8,256]{2,1,0:T(8,128)}, f32[2,8,256]{2,1,0:T(8,128)S(1)}, u32[]{:S(2)}, u32[]{:S(2)}) collective-permute-start(f32[2,8,256]{2,1,0:T(8,128)} %get-tuple-element.11), channel_id=1, source_target_pairs={{128,0},{256,128},{384,256},{0,384},{129,1},{257,129},{385,257},{1... | collective-permute-start | bytes 49160 | tf_op jit(solution)/shard_map/ppermute | solution.py:16
  18.1 10.2 %copy-start.3 = (f32[1,3,64,256]{3,2,1,0:T(8,128)S(1)}, f32[1,3,64,256]{3,2,1,0:T(8,128)}, u32[]{:S(2)}) copy-start(f32[1,3,64,256]{3,2,1,0:T(8,128)} %param.10) | copy-start | bytes 589828
  37.9 6.0 copy-start.1
  44.1 10.1 %copy-start.63 = (f32[66,8,256]{2,1,0:T(8,128)}, f32[66,8,256]{2,1,0:T(8,128)S(1)}, u32[]{:S(2)}) copy-start(f32[66,8,256]{2,1,0:T(8,128)S(1)} %get-tuple-element.9) | copy-start | bytes 1622020
  44.2 119.7 %collective-permute-start.2 = (f32[68,2,256]{2,0,1:T(8,128)S(1)}, f32[68,2,256]{2,0,1:T(8,128)S(1)}, u32[]{:S(2)}, u32[]{:S(2)}) collective-permute-start(f32[68,2,256]{2,0,1:T(8,128)S(1)} %copy.23), channel_id=1, source_target_pairs={{0,1},{1,2},{2,3},{3,4},{4,5},{5,6},{6,7},{7,8},{8,9},{9,10},{10,1... | collective-permute-start | bytes 417800 | tf_op jit(solution)/shard_map/ppermute | solution.py:13
  48.6 115.4 %collective-permute-start.3 = (f32[68,2,256]{2,0,1:T(8,128)}, f32[68,2,256]{2,0,1:T(8,128)}, u32[]{:S(2)}, u32[]{:S(2)}) collective-permute-start(f32[68,2,256]{2,0,1:T(8,128)} %copy.25), channel_id=1, source_target_pairs={{1,0},{2,1},{3,2},{4,3},{5,4},{6,5},{7,6},{8,7},{9,8},{10,9},{11,1... | collective-permute-start | bytes 417800 | tf_op jit(solution)/shard_map/ppermute | solution.py:16
  143.1 21.9 %copy-start = (f32[1,3,256,256]{3,2,1,0:T(8,128)S(1)}, f32[1,3,256,256]{3,2,1,0:T(8,128)}, u32[]{:S(2)}) copy-start(f32[1,3,256,256]{3,2,1,0:T(8,128)} %all_gather.7) | copy-start | bytes 2359300
  143.1 22.0 %copy-start.2 = (f32[64,8,256]{2,1,0:T(8,128)S(1)}, f32[64,8,256]{2,1,0:T(8,128)}, u32[]{:S(2)}) copy-start(f32[64,8,256]{2,1,0:T(8,128)} %param.6) | copy-start | bytes 1572868
  143.1 22.0 %copy-start.5 = (f32[68,8,256]{2,1,0:T(8,128)S(1)}, f32[68,8,256]{2,1,0:T(8,128)}, u32[]{:S(2)}) copy-start(f32[68,8,256]{2,1,0:T(8,128)} %copy-done.4) | copy-start | bytes 1671172
  143.1 22.0 %copy-start.35 = (f32[64]{0:T(128)S(1)}, f32[64]{0:T(128)}, u32[]{:S(2)}) copy-start(f32[64]{0:T(128)} %get-tuple-element.64) | copy-start | bytes 772
  143.1 22.0 %copy-start.36 = (f32[64]{0:T(128)S(1)}, f32[64]{0:T(128)}, u32[]{:S(2)}) copy-start(f32[64]{0:T(128)} %get-tuple-element.65) | copy-start | bytes 772
  143.1 22.0 %copy-start.37 = (f32[64]{0:T(128)S(1)}, f32[64]{0:T(128)}, u32[]{:S(2)}) copy-start(f32[64]{0:T(128)} %get-tuple-element.66) | copy-start | bytes 772
  143.1 22.0 %copy-start.38 = (f32[64]{0:T(128)S(1)}, f32[64]{0:T(128)}, u32[]{:S(2)}) copy-start(f32[64]{0:T(128)} %get-tuple-element.67) | copy-start | bytes 772
  143.1 22.0 %copy-start.55 = (f32[64]{0:T(128)S(1)}, f32[64]{0:T(128)}, u32[]{:S(2)}) copy-start(f32[64]{0:T(128)} %get-tuple-element.68) | copy-start | bytes 772
  143.2 22.0 %copy-start.56 = (f32[64]{0:T(128)S(1)}, f32[64]{0:T(128)}, u32[]{:S(2)}) copy-start(f32[64]{0:T(128)} %get-tuple-element.69) | copy-start | bytes 772
  143.2 22.0 %copy-start.57 = (f32[64]{0:T(128)S(1)}, f32[64]{0:T(128)}, u32[]{:S(2)}) copy-start(f32[64]{0:T(128)} %get-tuple-element.70) | copy-start | bytes 772
  143.2 22.0 %copy-start.58 = (f32[64]{0:T(128)S(1)}, f32[64]{0:T(128)}, u32[]{:S(2)}) copy-start(f32[64]{0:T(128)} %get-tuple-element.71) | copy-start | bytes 772
  143.2 22.0 %copy-start.59 = (f32[64]{0:T(128)S(1)}, f32[64]{0:T(128)}, u32[]{:S(2)}) copy-start(f32[64]{0:T(128)} %get-tuple-element.72) | copy-start | bytes 772
  143.2 22.0 %copy-start.60 = (f32[64]{0:T(128)S(1)}, f32[64]{0:T(128)}, u32[]{:S(2)}) copy-start(f32[64]{0:T(128)} %get-tuple-element.73) | copy-start | bytes 772
  143.2 22.0 %copy-start.61 = (f32[64]{0:T(128)S(1)}, f32[64]{0:T(128)}, u32[]{:S(2)}) copy-start(f32[64]{0:T(128)} %get-tuple-element.74) | copy-start | bytes 772
  143.2 22.0 %copy-start.62 = (f32[64]{0:T(128)S(1)}, f32[64]{0:T(128)}, u32[]{:S(2)}) copy-start(f32[64]{0:T(128)} %get-tuple-element.75) | copy-start | bytes 772
  165.2 5.1 copy-start.14
  165.2 5.1 copy-start.15
  165.2 5.1 copy-start.16
  165.2 5.1 copy-start.17
  165.2 5.1 copy-start.18
  165.2 5.1 copy-start.31
  165.3 5.1 copy-start.32
  165.3 5.1 copy-start.33
  165.3 5.1 copy-start.34
  165.3 5.1 copy-start.39
  165.3 5.1 copy-start.40
  165.3 5.1 copy-start.41
  165.3 5.1 copy-start.42
  165.3 5.1 copy-start.43
  165.3 5.1 copy-start.44
  165.3 5.1 copy-start.45
  165.4 5.1 copy-start.46
  165.4 5.1 copy-start.47
  165.4 5.1 copy-start.48
  165.4 5.1 copy-start.49
  165.4 5.1 copy-start.50
  165.4 5.1 copy-start.51
  165.4 5.1 copy-start.52
  176.3 436.3 %copy-start.8 = (f32[64]{0:T(128)S(1)}, f32[64]{0:T(128)}, u32[]{:S(2)}) copy-start(f32[64]{0:T(128)} %get-tuple-element.32) | copy-start | bytes 772
  176.3 436.3 %copy-start.9 = (f32[64]{0:T(128)S(1)}, f32[64]{0:T(128)}, u32[]{:S(2)}) copy-start(f32[64]{0:T(128)} %get-tuple-element.33) | copy-start | bytes 772
  176.3 436.4 %copy-start.10 = (f32[64]{0:T(128)S(1)}, f32[64]{0:T(128)}, u32[]{:S(2)}) copy-start(f32[64]{0:T(128)} %get-tuple-element.34) | copy-start | bytes 772
  176.3 436.4 %copy-start.11 = (f32[64]{0:T(128)S(1)}, f32[64]{0:T(128)}, u32[]{:S(2)}) copy-start(f32[64]{0:T(128)} %get-tuple-element.35) | copy-start | bytes 772
  176.3 436.4 %copy-start.12 = (f32[64]{0:T(128)S(1)}, f32[64]{0:T(128)}, u32[]{:S(2)}) copy-start(f32[64]{0:T(128)} %get-tuple-element.36) | copy-start | bytes 772
  176.3 436.4 %copy-start.13 = (f32[64]{0:T(128)S(1)}, f32[64]{0:T(128)}, u32[]{:S(2)}) copy-start(f32[64]{0:T(128)} %get-tuple-element.41) | copy-start | bytes 772
  176.3 436.4 %copy-start.19 = (f32[64]{0:T(128)S(1)}, f32[64]{0:T(128)}, u32[]{:S(2)}) copy-start(f32[64]{0:T(128)} %get-tuple-element.50) | copy-start | bytes 772
  176.3 436.4 %copy-start.20 = (f32[64]{0:T(128)S(1)}, f32[64]{0:T(128)}, u32[]{:S(2)}) copy-start(f32[64]{0:T(128)} %get-tuple-element.14) | copy-start | bytes 772
  176.3 436.4 %copy-start.21 = (f32[64]{0:T(128)S(1)}, f32[64]{0:T(128)}, u32[]{:S(2)}) copy-start(f32[64]{0:T(128)} %get-tuple-element.15) | copy-start | bytes 772
  176.3 436.4 %copy-start.22 = (f32[64]{0:T(128)S(1)}, f32[64]{0:T(128)}, u32[]{:S(2)}) copy-start(f32[64]{0:T(128)} %get-tuple-element.16) | copy-start | bytes 772
  176.4 436.4 %copy-start.23 = (f32[64]{0:T(128)S(1)}, f32[64]{0:T(128)}, u32[]{:S(2)}) copy-start(f32[64]{0:T(128)} %get-tuple-element.17) | copy-start | bytes 772
  176.4 436.4 %copy-start.24 = (f32[64]{0:T(128)S(1)}, f32[64]{0:T(128)}, u32[]{:S(2)}) copy-start(f32[64]{0:T(128)} %get-tuple-element.18) | copy-start | bytes 772
  176.4 436.4 %copy-start.25 = (f32[64]{0:T(128)S(1)}, f32[64]{0:T(128)}, u32[]{:S(2)}) copy-start(f32[64]{0:T(128)} %get-tuple-element.19) | copy-start | bytes 772
  176.4 436.4 %copy-start.26 = (f32[64]{0:T(128)S(1)}, f32[64]{0:T(128)}, u32[]{:S(2)}) copy-start(f32[64]{0:T(128)} %get-tuple-element.20) | copy-start | bytes 772
  176.4 436.4 %copy-start.27 = (f32[64]{0:T(128)S(1)}, f32[64]{0:T(128)}, u32[]{:S(2)}) copy-start(f32[64]{0:T(128)} %get-tuple-element.21) | copy-start | bytes 772
  176.4 436.4 %copy-start.28 = (f32[64]{0:T(128)S(1)}, f32[64]{0:T(128)}, u32[]{:S(2)}) copy-start(f32[64]{0:T(128)} %get-tuple-element.22) | copy-start | bytes 772
  176.4 436.4 %copy-start.29 = (f32[64]{0:T(128)S(1)}, f32[64]{0:T(128)}, u32[]{:S(2)}) copy-start(f32[64]{0:T(128)} %get-tuple-element.23) | copy-start | bytes 772
  176.4 436.4 %copy-start.30 = (f32[64]{0:T(128)S(1)}, f32[64]{0:T(128)}, u32[]{:S(2)}) copy-start(f32[64]{0:T(128)} %get-tuple-element.24) | copy-start | bytes 772
  (5 other events, 21.5 us)
Sparse Core Ops, SparseCore 0:
  9.4 598.2 all-gather.1
where the time goes:
time: 628 us; the launch traced here: 627 us
  waiting for transfers between devices  431 us (69%)
  local copies, waits for them, and re-layouts  119 us (19%)
  matrix products  22.7 us (4%)
  starting transfers between devices  16.4 us (3%)
  between operations  14.5 us (2%)
  other arithmetic  13.6 us (2%)
  blocking collectives  9.67 us (2%)
    all_gather x1, waiting for transfers between devices, polar_mix(): piece = lax.all_gather(sources, 'lon', axis=1, tiled=True)  431 us
    gather x2, local copies, waits for them, and re-layouts, polar_mix(): kernel = jnp.take(basis_half, gaps, axis=3)  108 us
    dot_general x3, matrix products, on_device(): jnp.dot(summed.reshape(-1, channels), mixing[basis_index], precision=lax....  17.9 us
  transfers between devices with their start and end apart: 5, of which 1 were waited for; matrix products, arithmetic and copies ran while one was open for 22% of the time, Pallas kernels for 0%

commit v1 on v0

v1 whole, which is shorter than its diff:
```python
import jax
import jax.numpy as jnp
from jax import lax
from jax.experimental import pallas as pl
from jax.experimental.pallas import tpu as pltpu
from jax.sharding import PartitionSpec as P

MESH = pl.DeviceIdType.MESH
F32 = jnp.float32
BF16 = jnp.bfloat16

ROWS, COLS, CH = 64, 8, 256
BASES = 3
TILE = 16
TILES = ROWS // TILE
GROUPS = (ROWS + 4) // 4
RING = 8
PLANE = 16
LON = RING * PLANE
LAT = 4


def split(x):
    hi = x.astype(BF16)
    return hi, (x - hi.astype(F32)).astype(BF16)


def dot3(a, b):
    def dot(x, y):
        return jnp.dot(x, y, preferred_element_type=F32)

    return dot(a[0], b[0]) + (dot(a[0], b[1]) + dot(a[1], b[0]))


def gelu(x):
    return 0.5 * x * (1.0 + lax.erf(x * 0.7071067811865476))


def iota(shape, dim):
    return lax.broadcasted_iota(jnp.int32, shape, dim)


def spread(ref, lead, row):
    return jnp.broadcast_to(ref[lead, pl.ds(row, 1), :], (8, 128))


def build_base(disc, wid, flip_main, flip_edge, main, edge):
    flip_main[...] = jnp.zeros_like(flip_main)
    flip_edge[...] = jnp.zeros_like(flip_edge)
    width = wid[...]
    for b in range(5):
        keep = (width >= abs(b - 2)).astype(F32)
        for k in range(BASES):
            for a in range(5):
                row = disc[a, b, k : k + 1, :] * keep
                at = (8 * a + b - 2) % 128
                flip_main[k, at : at + 1, 0:ROWS] = row
                if b < 2:
                    at = 32 + 2 * a + b
                    flip_edge[k, at : at + 1, 0:ROWS] = row
                if b > 2:
                    at = 65 + 2 * a + b - 3
                    flip_edge[k, at : at + 1, 0:ROWS] = row
    for k in range(BASES):
        main[k] = flip_main[k].T[0:ROWS]
        edge[k] = flip_edge[k].T[0:ROWS]


def build_band(main, edge, band):
    sub, lane = iota((8, 128), 0), iota((8, 128), 1)
    near = jnp.abs(lane % 8 - sub) <= 2
    side = ((sub < 2) & (lane < 64)) | ((sub >= 6) & (lane >= 64))
    odd = lane % 2 == 1
    fits = (sub == 0) | (sub == 7) | ((sub == 1) & odd) | ((sub == 6) & ~odd)
    low = lane < 32

    def step(n, carry):
        k, s = n // TILES, n % TILES
        for i in range(TILE):
            row = s * TILE + i
            m = pltpu.roll(spread(main, k, row), 8 * i, 1, stride=1, stride_axis=0)
            m = jnp.where(near, m, 0.0)
            h = jnp.where(side, spread(edge, k, row), 0.0)
            h = jnp.where(fits, pltpu.roll(h, 2 * i, 1, stride=1, stride_axis=0), 0.0)
            if i >= TILE - 4:
                h = jnp.where(low, m, h)
                m = jnp.where(low, 0.0, m)
            at = pl.multiple_of(k * TILE * 8, 8) + 8 * i
            band[s, pl.ds(at, 8), 0:128] = m
            band[s, pl.ds(at, 8), 128:256] = h
        return carry

    lax.fori_loop(0, BASES * TILES, step, 0)


def build_shifts(polar, rows, near, far, z):
    for k in range(BASES):
        for p in range(2):
            at = (2 * k + p) * 4
            rows[at : at + 4, :] = polar[k, p]
    lane = iota((24, 128), 1)
    parts = [rows[:, 128 * d : 128 * d + 128] for d in range(RING)]
    bits = [(lane // (8 * 2**b)) % 2 == 1 for b in range(3)]
    for b in range(3):
        turned = list(parts)
        for d in range(RING):
            if (d >> b) & 1 == 0:
                e = d + 2**b
                shift = 8 * 2**b
                turned[d] = jnp.where(bits[b], pltpu.roll(parts[e], shift, 1), parts[d])
                turned[e] = jnp.where(bits[b], parts[e], pltpu.roll(parts[d], 128 - shift, 1))
        parts = turned
    lower = lane < 64
    for t in range(PLANE):
        v = parts[t % 8]
        other = pltpu.roll(v, 64, 1)
        v = jnp.where(lower, v, other) if t < 8 else jnp.where(lower, other, v)
        here = pltpu.roll(v, 8 * z, 1)
        after = pltpu.roll(here, 8, 1)
        before = pltpu.roll(here, 120, 1)
        near[PLANE + t] = here
        near[t] = after
        far[PLANE + t] = before
        far[t] = here


def build_circular(near, far, circ, g, south):
    sub, lane = iota((8, 128), 0), iota((8, 128), 1)
    over = lane % 8 + sub >= 8
    last = (lane // 8) % 8 == 7
    upper = (lane >= 64) ^ (last & over)

    def step(out_g, carry):
        at = PLANE + g - out_g
        for k in range(BASES):
            for h in range(2):
                blocks = []
                for p in range(2):
                    first = (2 * k + p) * 4
                    q0 = first + 2 * h + south * (3 - 4 * h)
                    q1 = first + 2 * h + 1 + south * (1 - 4 * h)
                    a = jnp.where(upper, spread(near, at, q1), spread(near, at, q0))
                    b = jnp.where(upper, spread(far, at - 1, q1), spread(far, at - 1, q0))
                    v = jnp.where(over, b, a)
                    blocks.append(pltpu.roll(v, 0, 1, stride=1, stride_axis=0))
                circ[k, pl.ds(pl.multiple_of(out_g * 16, 16), 16), 128 * h : 128 * h + 128] = jnp.concatenate(blocks, axis=0)
        return carry

    lax.fori_loop(0, PLANE, step, 0)


def pack(xp, left, right):
    sub = iota((8, CH), 0)

    def place(rows, shifts):
        total = jnp.zeros((8, CH), F32)
        for r in range(4):
            if rows[r] is not None:
                moved = pltpu.roll(rows[r], shifts[r], 0) if shifts[r] else rows[r]
                total = jnp.where(sub // 2 == r, moved, total)
        return total

    def group(t, rows):
        left[t] = place(rows, (0, 2, 4, 6))
        right[t] = place(rows, (2, 4, 6, 0))

    group(0, [None, None, xp[2], xp[3]])
    group(GROUPS - 1, [xp[64], xp[65], None, None])

    def step(t, carry):
        group(t, [xp[4 * t + r] for r in range(4)])
        return carry

    lax.fori_loop(1, GROUPS - 1, step, 0)


def kernel(
    atm, disc_in, polar_in, wid_in, w_in, bias, out,
    xp, lsend, rsend, lrecv, rrecv, corner, disc, polar, wid, wall, whi, wlo,
    flip_main, flip_edge, main, edge, band, xz, prow, near, far, circ, mixp, rs, obuf,
    lsem, osem, halo_s, halo_r, wsem_s, wsem_r, zsem_s, zsem_r, rsem_s, rsem_r,
):
    lat, lon = lax.axis_index("lat"), lax.axis_index("lon")
    z, g = lon // PLANE, lon % PLANE
    before, after = (lon + LON - 1) % LON, (lon + 1) % LON
    sibling = lat + 1 - 2 * (lat % 2)
    across = ((lat + 2) % LAT, lon + 1 - 2 * (lon % 2))
    south = lat // (LAT - 1)
    has_up, has_down = lat > 0, lat < LAT - 1
    is_polar = (lat == 0) | (lat == LAT - 1)
    up, down = jnp.maximum(lat - 1, 0), jnp.minimum(lat + 1, LAT - 1)

    def local(src, dst, n):
        return pltpu.make_async_copy(src, dst, lsem.at[n])

    source_row = south * (ROWS - 4)
    load_x = local(atm, xp.at[pl.ds(2, ROWS)], 0)
    load_w = local(w_in.at[0], wall.at[:, pl.ds(pl.multiple_of(64 * lat, 64), 64)], 1)
    load_d = local(disc_in, disc, 2)
    load_wid = local(wid_in, wid, 3)
    load_p = local(polar_in.at[south], polar, 4)
    load_z = local(atm.at[pl.ds(source_row, 4)], xz.at[:, z], 5)
    for c in (load_x, load_d, load_wid, load_w):
        c.start()

    def remote(src, dst, s, r, device):
        return pltpu.make_async_remote_copy(src, dst, s, r, device_id=device, device_id_type=MESH)

    def ring(d):
        return (lat, ((z + d) % RING) * PLANE + g)

    def plane(d):
        return (lat, z * PLANE + (g + d) % PLANE)

    barrier = pltpu.get_barrier_semaphore()

    def greet(device):
        pl.semaphore_signal(barrier, inc=1, device_id=device, device_id_type=MESH)

    @pl.when(is_polar)
    def _():
        load_p.start()
        load_z.start()
        for d in range(1, RING):
            greet(ring(d))
        for d in range(1, PLANE):
            greet(plane(d))

    for device in ((lat, before), (lat, after), (sibling, lon), across):
        greet(device)

    @pl.when(has_up)
    def _():
        for column in (lon, before, after):
            greet((up, column))

    @pl.when(has_down)
    def _():
        for column in (lon, before, after):
            greet((down, column))

    load_x.wait()
    pack(xp, lsend, rsend)

    pl.semaphore_wait(barrier, 4 + 3 * (has_up.astype(jnp.int32) + has_down.astype(jnp.int32)) + 22 * is_polar.astype(jnp.int32))

    def gather(d):
        return remote(atm.at[pl.ds(source_row, 4)], xz.at[:, z], zsem_s.at[d], zsem_r.at[d], ring(d))

    def shard(n, source_lat, device):
        rows = pl.ds(pl.multiple_of(64 * source_lat, 64), 64)
        return remote(wall.at[:, rows], wall.at[:, rows], wsem_s.at[n], wsem_r.at[n], device)

    own_across = shard(0, lat, across)
    own_sibling = shard(1, lat, (sibling, lon))
    passed_on = shard(2, (lat + 2) % LAT, (sibling, lon))
    to_left = remote(lsend, rrecv, halo_s.at[0], halo_r.at[0], (lat, before))
    to_right = remote(rsend, lrecv, halo_s.at[1], halo_r.at[1], (lat, after))
    to_up = [
        remote(atm.at[pl.ds(0, 2)], xp.at[pl.ds(ROWS + 2, 2)], halo_s.at[2], halo_r.at[2], (up, lon)),
        remote(lsend.at[0], corner.at[3], halo_s.at[3], halo_r.at[3], (up, before)),
        remote(rsend.at[0], corner.at[2], halo_s.at[4], halo_r.at[4], (up, after)),
    ]
    to_down = [
        remote(atm.at[pl.ds(ROWS - 2, 2)], xp.at[pl.ds(0, 2)], halo_s.at[5], halo_r.at[5], (down, lon)),
        remote(lsend.at[GROUPS - 1], corner.at[1], halo_s.at[6], halo_r.at[6], (down, before)),
        remote(rsend.at[GROUPS - 1], corner.at[0], halo_s.at[7], halo_r.at[7], (down, after)),
    ]

    @pl.when(is_polar)
    def _():
        for d in (4, 3, 5, 2, 6, 1, 7):
            gather(d).start()

    load_w.wait()
    own_across.start()
    to_left.start()
    to_right.start()
    own_sibling.start()

    @pl.when(has_up)
    def _():
        for c in to_up:
            c.start()

    @pl.when(has_down)
    def _():
        for c in to_down:
            c.start()

    load_d.wait()
    load_wid.wait()
    build_base(disc, wid, flip_main, flip_edge, main, edge)
    build_band(main, edge, band)

    @pl.when(is_polar)
    def _():
        load_p.wait()
        build_shifts(polar, prow, near, far, z)
        build_circular(near, far, circ, g, south)

    own_across.wait_recv()
    passed_on.start()
    own_sibling.wait_recv()
    passed_on.wait_recv()
    for k in range(BASES):
        hi, lo = split(wall[k])
        whi[CH * k : CH * k + CH, :] = hi
        wlo[CH * k : CH * k + CH, :] = lo

    def mix(taps):
        return dot3(split(jnp.concatenate(taps, axis=1)), (whi[...], wlo[...]))

    def partial(d):
        rows = pl.ds(pl.multiple_of(16 * ((g + d) % PLANE), 16), 16)
        return remote(mixp.at[rows], rs.at[d], rsem_s.at[d], rsem_r.at[d], plane(d))

    @pl.when(is_polar)
    def _():
        load_z.wait()
        for d in range(1, RING):
            gather(d).wait_recv()
        sources = split(xz[...].reshape(CH, CH))
        mixp[...] = mix([dot3(split(circ[k]), sources) for k in range(BASES)])
        for d in (8, 7, 9, 6, 10, 5, 11, 4, 12, 3, 13, 2, 14, 1, 15):
            partial(d).start()

    to_left.wait_recv()
    to_right.wait_recv()
    sub = iota((8, CH), 0)

    @pl.when(has_up)
    def _():
        for c in to_down:
            c.wait_recv()
        lrecv[0] = jnp.where(sub < 4, corner[0], lrecv[0])
        rrecv[0] = jnp.where(sub < 4, corner[1], rrecv[0])

    @pl.when(jnp.logical_not(has_up))
    def _():
        xp[0:2] = jnp.zeros((2, COLS, CH), F32)

    @pl.when(has_down)
    def _():
        for c in to_up:
            c.wait_recv()
        lrecv[GROUPS - 1] = jnp.where(sub < 4, lrecv[GROUPS - 1], corner[2])
        rrecv[GROUPS - 1] = jnp.where(sub < 4, rrecv[GROUPS - 1], corner[3])

    @pl.when(jnp.logical_not(has_down))
    def _():
        xp[ROWS + 2 : ROWS + 4] = jnp.zeros((2, COLS, CH), F32)

    shift = bias[...]
    empty = jnp.zeros((16, CH), F32)
    stores = []

    def store(start, count, n):
        return pltpu.make_async_copy(obuf.at[pl.ds(start, count)], out.at[pl.ds(start, count)], osem.at[n])

    for s in range(TILES):
        x = jnp.concatenate(
            [
                xp[TILE * s : TILE * s + TILE + 4].reshape(160, CH),
                lrecv[4 * s : 4 * s + 5].reshape(40, CH),
                rrecv[4 * s : 4 * s + 5].reshape(40, CH),
                empty,
            ],
            axis=0,
        )
        taps = dot3(split(band[s]), split(x))
        mixed = mix([taps[128 * k : 128 * k + 128] for k in range(BASES)])
        obuf[TILE * s : TILE * s + TILE] = gelu(mixed + shift).reshape(TILE, COLS, CH)
        first, end = max(TILE * s, 2), min(TILE * s + TILE, ROWS - 2)
        stores.append(store(first, end - first, s))
        stores[-1].start()

    @pl.when(is_polar)
    def _():
        total = mixp[pl.ds(pl.multiple_of(16 * g, 16), 16), :]
        for d in range(1, PLANE):
            partial(d).wait_recv()
            total = total + rs[d]
        total = gelu(total + shift)
        for p in range(2):
            obuf[p + south * (ROWS - 1 - 2 * p)] = total[8 * p : 8 * p + 8]

    for start, n in ((0, TILES), (ROWS - 2, TILES + 1)):
        stores.append(store(start, 2, n))
        stores[-1].start()

    for c in (own_across, own_sibling, passed_on, to_left, to_right):
        c.wait_send()

    @pl.when(has_up)
    def _():
        for c in to_up:
            c.wait_send()

    @pl.when(has_down)
    def _():
        for c in to_down:
            c.wait_send()

    @pl.when(is_polar)
    def _():
        for d in range(1, RING):
            gather(d).wait_send()
        for d in range(1, PLANE):
            partial(d).wait_send()

    for c in stores:
        c.wait()


def on_device(atmosphere, disc_basis, polar_basis, widths, weights, channel_bias):
    anywhere = pl.BlockSpec(memory_space=pl.ANY)
    block = jax.ShapeDtypeStruct((ROWS, COLS, CH), F32)

    def vmem(*shape, dtype=F32):
        return pltpu.VMEM(shape, dtype)

    dma = pltpu.SemaphoreType.DMA
    return pl.pallas_call(
        kernel,
        out_shape=block,
        in_specs=[anywhere] * 5 + [pl.BlockSpec(memory_space=pltpu.VMEM)],
        out_specs=anywhere,
        scratch_shapes=[
            vmem(ROWS + 4, COLS, CH),
            vmem(GROUPS, 8, CH),
            vmem(GROUPS, 8, CH),
            vmem(GROUPS, 8, CH),
            vmem(GROUPS, 8, CH),
            vmem(4, 8, CH),
            vmem(5, 5, BASES, ROWS),
            vmem(BASES, 2, 4, 1024),
            vmem(1, ROWS, dtype=jnp.int32),
            vmem(BASES, CH, CH),
            vmem(BASES * CH, CH, dtype=BF16),
            vmem(BASES * CH, CH, dtype=BF16),
            vmem(BASES, 128, 128),
            vmem(BASES, 128, 128),
            vmem(BASES, ROWS, 128),
            vmem(BASES, ROWS, 128),
            vmem(TILES, BASES * TILE * 8, 256),
            vmem(4, RING, 8, CH),
            vmem(24, 1024),
            vmem(2 * PLANE, 24, 128),
            vmem(2 * PLANE, 24, 128),
            vmem(BASES, 256, 256),
            vmem(256, CH),
            vmem(PLANE, 16, CH),
            vmem(ROWS, COLS, CH),
            dma((6,)),
            dma((TILES + 2,)),
            dma((8,)),
            dma((8,)),
            dma((3,)),
            dma((3,)),
            dma((RING,)),
            dma((RING,)),
            dma((PLANE,)),
            dma((PLANE,)),
        ],
        compiler_params=pltpu.CompilerParams(
            collective_id=0, has_side_effects=True, vmem_limit_bytes=40 * 1024 * 1024
        ),
        name="disco",
    )(
        atmosphere,
        jnp.transpose(disc_basis, (2, 3, 0, 1)),
        polar_basis,
        widths.reshape(1, ROWS),
        weights,
        channel_bias,
    )


def solution(mesh):
    return jax.shard_map(
        on_device,
        mesh=mesh,
        in_specs=(
            P("lat", "lon", None),
            P(None, "lat", None, None),
            P(),
            P("lat"),
            P(None, None, "lat", None),
            P(),
        ),
        out_specs=P("lat", "lon", None),
        check_vma=False,
    )
```

time: 628 us -> 34.4 us (0.05)
  the two profiles are of different devices: /device:TPU:6 before, /device:TPU:8 now
where the time goes in v1:
time: 34.4 us; the launch traced here: 34.2 us
  Pallas kernels  29 us (84%)
  local copies, waits for them, and re-layouts  5.17 us (15%)
    pallas_call x1, Pallas kernels, on_device(): pl.pallas_call(kernel, out_shape=block, in_specs=[anywhere] * 5 + [pl.Blo...  29 us
    unnamed x13, local copies, waits for them, and re-layouts  5.17 us

profile of v1, /device:TPU:8, one launch (start us, length us, event | category | flops | bytes accessed | tf_op | source)
XLA Modules:
  0.0 34.2 jit_solution(2030250844250576098)
XLA Ops:
  0.0 0.0 copy-start.4
  0.0 0.0 copy-start.5
  0.0 0.7 %copy-done.4 = f32[1,256]{1,0:T(1,128)S(1)} copy-done((f32[1,256]{1,0:T(1,128)S(1)}, f32[1,256]{1,0:T(1,128)}, u32[]{:S(2)}) %copy-start.4) | copy-done | bytes 1048
  0.7 0.0 copy-done.5
  0.7 0.0 copy-start
  0.7 1.0 %copy-done = f32[64,8,256]{2,1,0:T(8,128)S(1)} copy-done((f32[64,8,256]{2,1,0:T(8,128)S(1)}, f32[64,8,256]{2,1,0:T(8,128)}, u32[]{:S(2)}) %copy-start) | copy-done | bytes 524312
  1.7 0.0 copy-start.1
  1.7 0.9 %copy-done.1 = f32[2,3,2,4,1024]{4,3,2,1,0:T(4,128)S(1)} copy-done((f32[2,3,2,4,1024]{4,3,2,1,0:T(4,128)S(1)}, f32[2,3,2,4,1024]{4,3,2,1,0:T(4,128)}, u32[]{:S(2)}) %copy-start.1) | copy-done | bytes 196632
  2.7 0.0 copy-start.2
  2.7 0.9 %copy-done.2 = f32[1,3,64,256]{3,2,1,0:T(8,128)S(1)} copy-done((f32[1,3,64,256]{3,2,1,0:T(8,128)S(1)}, f32[1,3,64,256]{3,2,1,0:T(8,128)}, u32[]{:S(2)}) %copy-start.2) | copy-done | bytes 196632
  3.6 0.0 copy-start.3
  3.6 0.8 %copy-done.3 = f32[3,64,5,5]{1,0,3,2:T(4,128)S(1)} copy-done((f32[3,64,5,5]{1,0,3,2:T(4,128)S(1)}, f32[3,64,5,5]{1,0,3,2:T(4,128)}, u32[]{:S(2)}) %copy-start.3) | copy-done | bytes 19224
  4.4 29.0 %disco.1 = f32[64,8,256]{2,1,0:T(8,128)S(1)} custom-call(f32[64,8,256]{2,1,0:T(8,128)S(1)} %copy-done, f32[5,5,3,64]{3,2,1,0:T(4,128)S(1)} %bitcast.2, f32[2,3,2,4,1024]{4,3,2,1,0:T(4,128)S(1)} %copy-done.1, s32[1,64]{1,0:T(1,128)S(1)} %bitcast.3, f32[1,3,64,256]{3,2,1,0:T(8,128)S(1)} %copy-done.2, f32[1,256]{1,0:T(1,128)S(1)} %copy-done.4), custom_call_target="tpu_custom_call" | custom-call | tf_op jit(solution)/shard_map/disco/pallas_call | solution.py:424
  33.4 0.8 %copy.8 = f32[64,8,256]{2,1,0:T(8,128)} copy(f32[64,8,256]{2,1,0:T(8,128)S(1)} %disco.1) | data formatting | bytes 1048576
Async XLA Ops:
  0.0 0.7 %copy-start.4 = (f32[1,256]{1,0:T(1,128)S(1)}, f32[1,256]{1,0:T(1,128)}, u32[]{:S(2)}) copy-start(f32[1,256]{1,0:T(1,128)} %bias.1) | copy-start | bytes 3076
  0.0 0.7 %copy-start.5 = (s32[64]{0:T(128)S(1)}, s32[64]{0:T(128)}, u32[]{:S(2)}) copy-start(s32[64]{0:T(128)} %param.9) | copy-start | bytes 772
  0.7 1.0 %copy-start = (f32[64,8,256]{2,1,0:T(8,128)S(1)}, f32[64,8,256]{2,1,0:T(8,128)}, u32[]{:S(2)}) copy-start(f32[64,8,256]{2,1,0:T(8,128)} %atm.1) | copy-start | bytes 1572868
  1.7 0.9 %copy-start.1 = (f32[2,3,2,4,1024]{4,3,2,1,0:T(4,128)S(1)}, f32[2,3,2,4,1024]{4,3,2,1,0:T(4,128)}, u32[]{:S(2)}) copy-start(f32[2,3,2,4,1024]{4,3,2,1,0:T(4,128)} %polar_in.1) | copy-start | bytes 589828
  2.7 0.9 %copy-start.2 = (f32[1,3,64,256]{3,2,1,0:T(8,128)S(1)}, f32[1,3,64,256]{3,2,1,0:T(8,128)}, u32[]{:S(2)}) copy-start(f32[1,3,64,256]{3,2,1,0:T(8,128)} %w_in.1) | copy-start | bytes 589828
  3.6 0.8 %copy-start.3 = (f32[3,64,5,5]{1,0,3,2:T(4,128)S(1)}, f32[3,64,5,5]{1,0,3,2:T(4,128)}, u32[]{:S(2)}) copy-start(f32[3,64,5,5]{1,0,3,2:T(4,128)} %param.7) | copy-start | bytes 57604

commit v2 on v1

--- a/solution.py
+++ b/solution.py
@@ -124,14 +124,18 @@
         far[t] = here
 
 
-def build_circular(near, far, circ, g, south):
+def distance(n):
+    return PLANE // 2 + (n + 1) // 2 * (1 - 2 * (n % 2))
+
+
+def build_circular(near, far, chi, clo, g, south):
     sub, lane = iota((8, 128), 0), iota((8, 128), 1)
     over = lane % 8 + sub >= 8
     last = (lane // 8) % 8 == 7
     upper = (lane >= 64) ^ (last & over)
 
-    def step(out_g, carry):
-        at = PLANE + g - out_g
+    def step(n, carry):
+        at = PLANE + g - (g + distance(n)) % PLANE
         for k in range(BASES):
             for h in range(2):
                 blocks = []
@@ -143,7 +147,10 @@
                     b = jnp.where(upper, spread(far, at - 1, q1), spread(far, at - 1, q0))
                     v = jnp.where(over, b, a)
                     blocks.append(pltpu.roll(v, 0, 1, stride=1, stride_axis=0))
-                circ[k, pl.ds(pl.multiple_of(out_g * 16, 16), 16), 128 * h : 128 * h + 128] = jnp.concatenate(blocks, axis=0)
+                rows = pl.ds(pl.multiple_of(n * 16, 16), 16)
+                hi, lo = split(jnp.concatenate(blocks, axis=0))
+                chi[k, rows, 128 * h : 128 * h + 128] = hi
+                clo[k, rows, 128 * h : 128 * h + 128] = lo
         return carry
 
     lax.fori_loop(0, PLANE, step, 0)
@@ -175,10 +182,10 @@
 
 
 def kernel(
-    atm, disc_in, polar_in, wid_in, w_in, bias, out,
-    xp, lsend, rsend, lrecv, rrecv, corner, disc, polar, wid, wall, whi, wlo,
-    flip_main, flip_edge, main, edge, band, xz, prow, near, far, circ, mixp, rs, obuf,
-    lsem, osem, halo_s, halo_r, wsem_s, wsem_r, zsem_s, zsem_r, rsem_s, rsem_r,
+    atm, disc_in, polar_in, wid_in, w_in, bias_in, out,
+    xp, lsend, rsend, lrecv, rrecv, corner, disc, polar, wid, bias, wall, whi, wlo,
+    flip_main, flip_edge, main, edge, band, xz, prow, near, far, chi, clo, mixp, rs,
+    lsem, halo_s, halo_r, wsem_s, wsem_r, zsem_s, zsem_r, rsem_s, rsem_r,
 ):
     lat, lon = lax.axis_index("lat"), lax.axis_index("lon")
     z, g = lon // PLANE, lon % PLANE
@@ -187,6 +194,7 @@
     across = ((lat + 2) % LAT, lon + 1 - 2 * (lon % 2))
     south = lat // (LAT - 1)
     has_up, has_down = lat > 0, lat < LAT - 1
+    first, last = lon == 0, lon == LON - 1
     is_polar = (lat == 0) | (lat == LAT - 1)
     up, down = jnp.maximum(lat - 1, 0), jnp.minimum(lat + 1, LAT - 1)
 
@@ -199,9 +207,8 @@
     load_d = local(disc_in, disc, 2)
     load_wid = local(wid_in, wid, 3)
     load_p = local(polar_in.at[south], polar, 4)
+    load_b = local(bias_in, bias, 6)
     load_z = local(atm.at[pl.ds(source_row, 4)], xz.at[:, z], 5)
-    for c in (load_x, load_d, load_wid, load_w):
-        c.start()
 
     def remote(src, dst, s, r, device):
         return pltpu.make_async_remote_copy(src, dst, s, r, device_id=device, device_id_type=MESH)
@@ -217,43 +224,85 @@
     def greet(device):
         pl.semaphore_signal(barrier, inc=1, device_id=device, device_id_type=MESH)
 
+    early = z < RING // 2
+
+    def early_at(d):
+        return (z + d) % RING < RING // 2
+
     @pl.when(is_polar)
     def _():
+        for n in range(PLANE - 1):
+            greet(plane(distance(n)))
+
+    for device in ((sibling, lon), across, (lat, before)):
+        greet(device)
+
+    @pl.when(jnp.logical_not(last))
+    def _():
+        greet((lat, after))
+
+    for there, row in ((has_up, up), (has_down, down)):
+
+        @pl.when(there)
+        def _(row=row):
+            greet((row, lon))
+            greet((row, before))
+
+        @pl.when(there & jnp.logical_not(last))
+        def _(row=row):
+            greet((row, after))
+
+    @pl.when(is_polar)
+    def _():
+        for d in range(1, RING):
+
+            @pl.when(early | jnp.logical_not(early_at(d)))
+            def _(d=d):
+                greet(ring(d))
+
         load_p.start()
         load_z.start()
-        for d in range(1, RING):
-            greet(ring(d))
-        for d in range(1, PLANE):
-            greet(plane(d))
-
-    for device in ((lat, before), (lat, after), (sibling, lon), across):
-        greet(device)
-
-    @pl.when(has_up)
-    def _():
-        for column in (lon, before, after):
-            greet((up, column))
-
-    @pl.when(has_down)
-    def _():
-        for column in (lon, before, after):
-            greet((down, column))
-
-    load_x.wait()
-    pack(xp, lsend, rsend)
-
-    pl.semaphore_wait(barrier, 4 + 3 * (has_up.astype(jnp.int32) + has_down.astype(jnp.int32)) + 22 * is_polar.astype(jnp.int32))
+
+    for c in (load_x, load_d, load_wid, load_w, load_b):
+        c.start()
+
+    def prepare():
+        load_d.wait()
+        load_wid.wait()
+        build_base(disc, wid, flip_main, flip_edge, main, edge)
+        build_band(main, edge, band)
+
+        @pl.when(is_polar)
+        def _():
+            load_p.wait()
+            build_shifts(polar, prow, near, far, z)
+            build_circular(near, far, chi, clo, g, south)
+
+    @pl.when(early)
+    def _():
+        load_x.wait()
+        pack(xp, lsend, rsend)
+        prepare()
+
+    def count(condition):
+        return condition.astype(jnp.int32)
+
+    pl.semaphore_wait(
+        barrier,
+        4 - count(first) + (3 - count(first)) * (count(has_up) + count(has_down)) + (PLANE + 6 - 4 * count(early)) * count(is_polar),
+    )
 
     def gather(d):
         return remote(atm.at[pl.ds(source_row, 4)], xz.at[:, z], zsem_s.at[d], zsem_r.at[d], ring(d))
 
-    def shard(n, source_lat, device):
+    def shard(k, n, source_lat, device):
         rows = pl.ds(pl.multiple_of(64 * source_lat, 64), 64)
-        return remote(wall.at[:, rows], wall.at[:, rows], wsem_s.at[n], wsem_r.at[n], device)
-
-    own_across = shard(0, lat, across)
-    own_sibling = shard(1, lat, (sibling, lon))
-    passed_on = shard(2, (lat + 2) % LAT, (sibling, lon))
+        source = wall.at[k, rows] if n == 2 else w_in.at[0, k]
+        return remote(source, wall.at[k, rows], wsem_s.at[k, n], wsem_r.at[k, n], device)
+
+    own_across = [shard(k, 0, lat, across) for k in range(BASES)]
+    own_sibling = [shard(k, 1, lat, (sibling, lon)) for k in range(BASES)]
+    passed_on = [shard(k, 2, (lat + 2) % LAT, (sibling, lon)) for k in range(BASES)]
     to_left = remote(lsend, rrecv, halo_s.at[0], halo_r.at[0], (lat, before))
     to_right = remote(rsend, lrecv, halo_s.at[1], halo_r.at[1], (lat, after))
     to_up = [
@@ -270,69 +319,98 @@
     @pl.when(is_polar)
     def _():
         for d in (4, 3, 5, 2, 6, 1, 7):
-            gather(d).start()
+
+            @pl.when(early_at(d) | jnp.logical_not(early))
+            def _(d=d):
+                gather(d).start()
+
+    for c in own_across:
+        c.start()
+
+    @pl.when(jnp.logical_not(early))
+    def _():
+        load_x.wait()
+        pack(xp, lsend, rsend)
+
+    to_right.start()
+
+    @pl.when(jnp.logical_not(first))
+    def _():
+        to_left.start()
+
+    for c in own_sibling:
+        c.start()
+
+    for there, copies in ((has_up, to_up), (has_down, to_down)):
+
+        @pl.when(there)
+        def _(copies=copies):
+            copies[0].start()
+            copies[2].start()
+
+        @pl.when(there & jnp.logical_not(first))
+        def _(copies=copies):
+            copies[1].start()
+
+    @pl.when(jnp.logical_not(early))
+    def _():
+        prepare()
+
+    for c, d in zip(own_across, passed_on):
+        c.wait_recv()
+        d.start()
 
     load_w.wait()
-    own_across.start()
-    to_left.start()
-    to_right.start()
-    own_sibling.start()
-
-    @pl.when(has_up)
-    def _():
-        for c in to_up:
-            c.start()
-
-    @pl.when(has_down)
-    def _():
-        for c in to_down:
-            c.start()
-
-    load_d.wait()
-    load_wid.wait()
-    build_base(disc, wid, flip_main, flip_edge, main, edge)
-    build_band(main, edge, band)
-
-    @pl.when(is_polar)
-    def _():
-        load_p.wait()
-        build_shifts(polar, prow, near, far, z)
-        build_circular(near, far, circ, g, south)
-
-    own_across.wait_recv()
-    passed_on.start()
-    own_sibling.wait_recv()
-    passed_on.wait_recv()
     for k in range(BASES):
+        own_sibling[k].wait_recv()
+        passed_on[k].wait_recv()
         hi, lo = split(wall[k])
         whi[CH * k : CH * k + CH, :] = hi
         wlo[CH * k : CH * k + CH, :] = lo
 
     def mix(taps):
-        return dot3(split(jnp.concatenate(taps, axis=1)), (whi[...], wlo[...]))
-
-    def partial(d):
-        rows = pl.ds(pl.multiple_of(16 * ((g + d) % PLANE), 16), 16)
-        return remote(mixp.at[rows], rs.at[d], rsem_s.at[d], rsem_r.at[d], plane(d))
+        return dot3(split(taps), (whi[...], wlo[...]))
+
+    def partial(n):
+        d = distance(n)
+        return remote(mixp.at[pl.ds(16 * n, 16)], rs.at[n], rsem_s.at[n], rsem_r.at[n], plane(d))
 
     @pl.when(is_polar)
     def _():
         load_z.wait()
-        for d in range(1, RING):
+        for d in (4, 5, 3, 6, 2, 7, 1):
             gather(d).wait_recv()
+
+            @pl.when(early & jnp.logical_not(early_at(RING - d)))
+            def _(d=d):
+                gather(RING - d).start()
+
         sources = split(xz[...].reshape(CH, CH))
-        mixp[...] = mix([dot3(split(circ[k]), sources) for k in range(BASES)])
-        for d in (8, 7, 9, 6, 10, 5, 11, 4, 12, 3, 13, 2, 14, 1, 15):
-            partial(d).start()
+        for half in range(2):
+            rows = slice(128 * half, 128 * half + 128)
+            taps = [dot3((chi[k, rows], clo[k, rows]), sources) for k in range(BASES)]
+            mixp[rows] = mix(jnp.concatenate(taps, axis=1))
+            for n in range(8 * half, min(8 * half + 8, PLANE - 1)):
+                partial(n).start()
+
+    to_right.wait_recv()
+
+    @pl.when(first)
+    def _():
+        to_left.start()
 
     to_left.wait_recv()
-    to_right.wait_recv()
     sub = iota((8, CH), 0)
 
     @pl.when(has_up)
     def _():
         for c in to_down:
             c.wait_recv()
+
+        @pl.when(first)
+        def _():
+            to_up[1].start()
+
         lrecv[0] = jnp.where(sub < 4, corner[0], lrecv[0])
         rrecv[0] = jnp.where(sub < 4, corner[1], rrecv[0])
 
@@ -344,6 +422,11 @@
     def _():
         for c in to_up:
             c.wait_recv()
+
+        @pl.when(first)
+        def _():
+            to_down[1].start()
+
         lrecv[GROUPS - 1] = jnp.where(sub < 4, lrecv[GROUPS - 1], corner[2])
         rrecv[GROUPS - 1] = jnp.where(sub < 4, rrecv[GROUPS - 1], corner[3])
 
@@ -351,13 +434,9 @@
     def _():
         xp[ROWS + 2 : ROWS + 4] = jnp.zeros((2, COLS, CH), F32)
 
+    load_b.wait()
     shift = bias[...]
     empty = jnp.zeros((16, CH), F32)
-    stores = []
-
-    def store(start, count, n):
-        return pltpu.make_async_copy(obuf.at[pl.ds(start, count)], out.at[pl.ds(start, count)], osem.at[n])
-
     for s in range(TILES):
         x = jnp.concatenate(
             [
@@ -368,28 +447,21 @@
             ],
             axis=0,
         )
-        taps = dot3(split(band[s]), split(x))
-        mixed = mix([taps[128 * k : 128 * k + 128] for k in range(BASES)])
-        obuf[TILE * s : TILE * s + TILE] = gelu(mixed + shift).reshape(TILE, COLS, CH)
-        first, end = max(TILE * s, 2), min(TILE * s + TILE, ROWS - 2)
-        stores.append(store(first, end - first, s))
-        stores[-1].start()
+        tile = dot3(split(band[s]), split(x))
+        mixed = mix(jnp.concatenate([tile[128 * k : 128 * k + 128] for k in range(BASES)], axis=1))
+        out[TILE * s : TILE * s + TILE] = gelu(mixed + shift).reshape(TILE, COLS, CH)
 
     @pl.when(is_polar)
     def _():
-        total = mixp[pl.ds(pl.multiple_of(16 * g, 16), 16), :]
-        for d in range(1, PLANE):
-            partial(d).wait_recv()
-            total = total + rs[d]
+        total = mixp[16 * PLANE - 16 : 16 * PLANE, :]
+        for n in range(PLANE - 1):
+            partial(n).wait_recv()
+            total = total + rs[n]
         total = gelu(total + shift)
         for p in range(2):
-            obuf[p + south * (ROWS - 1 - 2 * p)] = total[8 * p : 8 * p + 8]
-
-    for start, n in ((0, TILES), (ROWS - 2, TILES + 1)):
-        stores.append(store(start, 2, n))
-        stores[-1].start()
-
-    for c in (own_across, own_sibling, passed_on, to_left, to_right):
+            out[p + south * (ROWS - 1 - 2 * p)] = total[8 * p : 8 * p + 8]
+
+    for c in own_across + own_sibling + passed_on + [to_left, to_right]:
         c.wait_send()
 
     @pl.when(has_up)
@@ -406,16 +478,16 @@
     def _():
         for d in range(1, RING):
             gather(d).wait_send()
-        for d in range(1, PLANE):
-            partial(d).wait_send()
-
-    for c in stores:
-        c.wait()
+        for n in range(PLANE - 1):
+            partial(n).wait_send()
 
 
 def on_device(atmosphere, disc_basis, polar_basis, widths, weights, channel_bias):
-    anywhere = pl.BlockSpec(memory_space=pl.ANY)
-    block = jax.ShapeDtypeStruct((ROWS, COLS, CH), F32)
+    anywhere = pl.BlockSpec(memory_space=pltpu.MemorySpace.HBM)
+
+    def in_hbm(x):
+        return pltpu.with_memory_space_constraint(x, pltpu.MemorySpace.HBM)
+
 
     def vmem(*shape, dtype=F32):
         return pltpu.VMEM(shape, dtype)
@@ -423,9 +495,9 @@
     dma = pltpu.SemaphoreType.DMA
     return pl.pallas_call(
         kernel,
-        out_shape=block,
-        in_specs=[anywhere] * 5 + [pl.BlockSpec(memory_space=pltpu.VMEM)],
-        out_specs=anywhere,
+        out_shape=pltpu.VMEM((ROWS, COLS, CH), F32),
+        in_specs=[anywhere] * 6,
+        out_specs=pl.BlockSpec(memory_space=pltpu.VMEM),
         scratch_shapes=[
             vmem(ROWS + 4, COLS, CH),
             vmem(GROUPS, 8, CH),
@@ -436,6 +508,7 @@
             vmem(5, 5, BASES, ROWS),
             vmem(BASES, 2, 4, 1024),
             vmem(1, ROWS, dtype=jnp.int32),
+            vmem(1, CH),
             vmem(BASES, CH, CH),
             vmem(BASES * CH, CH, dtype=BF16),
             vmem(BASES * CH, CH, dtype=BF16),
@@ -448,32 +521,31 @@
             vmem(24, 1024),
             vmem(2 * PLANE, 24, 128),
             vmem(2 * PLANE, 24, 128),
-            vmem(BASES, 256, 256),
+            vmem(BASES, 256, 256, dtype=BF16),
+            vmem(BASES, 256, 256, dtype=BF16),
             vmem(256, CH),
             vmem(PLANE, 16, CH),
-            vmem(ROWS, COLS, CH),
-            dma((6,)),
-            dma((TILES + 2,)),
+            dma((7,)),
             dma((8,)),
             dma((8,)),
-            dma((3,)),
-            dma((3,)),
+            dma((BASES, 3)),
+            dma((BASES, 3)),
             dma((RING,)),
             dma((RING,)),
             dma((PLANE,)),
             dma((PLANE,)),
         ],
         compiler_params=pltpu.CompilerParams(
-            collective_id=0, has_side_effects=True, vmem_limit_bytes=40 * 1024 * 1024
+            collective_id=0, has_side_effects=True, vmem_limit_bytes=32 * 1024 * 1024
         ),
         name="disco",
     )(
-        atmosphere,
-        jnp.transpose(disc_basis, (2, 3, 0, 1)),
-        polar_basis,
-        widths.reshape(1, ROWS),
-        weights,
-        channel_bias,
+        in_hbm(atmosphere),
+        in_hbm(jnp.transpose(disc_basis, (2, 3, 0, 1))),
+        in_hbm(polar_basis),
+        in_hbm(widths.reshape(1, ROWS)),
+        in_hbm(weights),
+        in_hbm(channel_bias),
     )
 
 

time: 34.4 us -> 29.2 us (0.85)
  local copies, waits for them, and re-layouts: 5.17 us -> 0.8 us
  Pallas kernels: 29 us -> 28.3 us
    unnamed x13 -> x1, local copies, waits for them, and re-layouts: 5.17 us -> 0.8 us
    pallas_call x1, Pallas kernels: 29 us -> 28.3 us  [on_device(): pl.pallas_call(kernel, out_shape=pltpu.VMEM((ROWS, COLS, CH), F32), in_sp...]
where the time goes in v2:
time: 29.2 us; the launch traced here: 29.1 us
  Pallas kernels  28.3 us (97%)
  local copies, waits for them, and re-layouts  0.8 us (3%)
    pallas_call x1, Pallas kernels, on_device(): pl.pallas_call(kernel, out_shape=pltpu.VMEM((ROWS, COLS, CH), F32), in_sp...  28.3 us
    unnamed x1, local copies, waits for them, and re-layouts  0.8 us

profile of v2, /device:TPU:8, one launch (start us, length us, event | category | flops | bytes accessed | tf_op | source)
XLA Modules:
  0.0 29.1 jit_solution(2332895448018022998)
XLA Ops:
  0.0 28.3 %disco.1 = f32[64,8,256]{2,1,0:T(8,128)S(1)} custom-call(f32[64,8,256]{2,1,0:T(8,128)} %atm.1, f32[5,5,3,64]{3,2,1,0:T(4,128)} %bitcast.2, f32[2,3,2,4,1024]{4,3,2,1,0:T(4,128)} %polar_in.1, s32[1,64]{1,0:T(1,128)} %bitcast.3, f32[1,3,64,256]{3,2,1,0:T(8,128)} %w_in.1, f32[1,256]{1,0:T(1,128)} %bias_in.1), custom_call_target="tpu_custom_call" | custom-call | tf_op jit(solution)/shard_map/disco/pallas_call | solution.py:496
  28.3 0.8 %copy.8 = f32[64,8,256]{2,1,0:T(8,128)} copy(f32[64,8,256]{2,1,0:T(8,128)S(1)} %disco.1) | data formatting | bytes 1048576

commit v3 on v2

--- a/solution.py
+++ b/solution.py
@@ -184,8 +184,8 @@
 def kernel(
     atm, disc_in, polar_in, wid_in, w_in, bias_in, out,
     xp, lsend, rsend, lrecv, rrecv, corner, disc, polar, wid, bias, wall, whi, wlo,
-    flip_main, flip_edge, main, edge, band, xz, prow, near, far, chi, clo, mixp, rs,
-    lsem, halo_s, halo_r, wsem_s, wsem_r, zsem_s, zsem_r, rsem_s, rsem_r,
+    flip_main, flip_edge, main, edge, band, xz, prow, shift_a, shift_b, chi, clo, mixp, rs,
+    lsem, halo_s, halo_r, wsem_s, wsem_r, zsem_s, zsem_r, rsem_s, rsem_r, known, hello, near, seam,
 ):
     lat, lon = lax.axis_index("lat"), lax.axis_index("lon")
     z, g = lon // PLANE, lon % PLANE
@@ -224,76 +224,79 @@
     def greet(device):
         pl.semaphore_signal(barrier, inc=1, device_id=device, device_id_type=MESH)
 
-    early = z < RING // 2
-
-    def early_at(d):
-        return (z + d) % RING < RING // 2
-
-    @pl.when(is_polar)
-    def _():
-        for n in range(PLANE - 1):
-            greet(plane(distance(n)))
-
-    for device in ((sibling, lon), across, (lat, before)):
-        greet(device)
-
-    @pl.when(jnp.logical_not(last))
-    def _():
-        greet((lat, after))
-
-    for there, row in ((has_up, up), (has_down, down)):
+    late = z >= RING // 2
+    turn = PLANE - 1 - 2 * g
+    turning = is_polar & ((g == 0) | (g == PLANE - 1))
+    odd = lon % 2 == 1
+    whole = lon >= 0
+
+    neighbours = [
+        (jnp.logical_not(last), whole, (lat, after)),
+        (jnp.logical_not(first), jnp.logical_not(whole), (lat, before)),
+        (has_up, jnp.logical_not(whole), (up, lon)),
+        (has_down, whole, (down, lon)),
+        (has_up & jnp.logical_not(last), whole, (up, after)),
+        (has_down & jnp.logical_not(last), whole, (down, after)),
+        (has_up & jnp.logical_not(first), jnp.logical_not(whole), (up, before)),
+        (has_down & jnp.logical_not(first), jnp.logical_not(whole), (down, before)),
+        (whole, jnp.logical_not(odd), across),
+        (turning, g == 0, (lat, lon + turn)),
+    ]
+
+    def count(*conditions):
+        return sum(c.astype(jnp.int32) for c in conditions)
+
+    @pl.when(is_polar)
+    def _():
+        load_z.start()
+
+    for there, later, device in neighbours:
+
+        @pl.when(there & later)
+        def _(device=device):
+            greet(device)
+
+    for there, row in ((first, lat), (first & has_up, up), (first & has_down, down)):
 
         @pl.when(there)
         def _(row=row):
-            greet((row, lon))
             greet((row, before))
 
-        @pl.when(there & jnp.logical_not(last))
-        def _(row=row):
-            greet((row, after))
-
     @pl.when(is_polar)
     def _():
         for d in range(1, RING):
 
-            @pl.when(early | jnp.logical_not(early_at(d)))
+            @pl.when(z + d < RING)
             def _(d=d):
                 greet(ring(d))
 
         load_p.start()
-        load_z.start()
 
     for c in (load_x, load_d, load_wid, load_w, load_b):
         c.start()
 
-    def prepare():
+    def prepare_base():
         load_d.wait()
         load_wid.wait()
         build_base(disc, wid, flip_main, flip_edge, main, edge)
+
+    def prepare_band():
         build_band(main, edge, band)
 
-        @pl.when(is_polar)
-        def _():
-            load_p.wait()
-            build_shifts(polar, prow, near, far, z)
-            build_circular(near, far, chi, clo, g, south)
-
-    @pl.when(early)
-    def _():
-        load_x.wait()
-        pack(xp, lsend, rsend)
-        prepare()
-
-    def count(condition):
-        return condition.astype(jnp.int32)
-
-    pl.semaphore_wait(
-        barrier,
-        4 - count(first) + (3 - count(first)) * (count(has_up) + count(has_down)) + (PLANE + 6 - 4 * count(early)) * count(is_polar),
-    )
+    def prepare_polar():
+        load_p.wait()
+        build_shifts(polar, prow, shift_a, shift_b, z)
+        build_circular(shift_a, shift_b, chi, clo, g, south)
+
+    greeted = count(*[there & jnp.logical_not(later) for there, later, _ in neighbours])
+    greeted += count(last, last & has_up, last & has_down) + z * count(is_polar)
+
+    @pl.when(greeted > 0)
+    def _():
+        pl.semaphore_wait(barrier, greeted)
 
     def gather(d):
-        return remote(atm.at[pl.ds(source_row, 4)], xz.at[:, z], zsem_s.at[d], zsem_r.at[d], ring(d))
+        return remote(xz.at[:, z], xz.at[:, z], zsem_s.at[d], zsem_r.at[d], ring(d))
 
     def shard(k, n, source_lat, device):
         rows = pl.ds(pl.multiple_of(64 * source_lat, 64), 64)
@@ -318,23 +321,56 @@
 
     @pl.when(is_polar)
     def _():
+        for d in range(1, RING):
+
+            @pl.when(z + d >= RING)
+            def _(d=d):
+                pl.semaphore_signal(hello.at[d], inc=1, device_id=ring(d), device_id_type=MESH)
+
+        load_z.wait()
         for d in (4, 3, 5, 2, 6, 1, 7):
 
-            @pl.when(early_at(d) | jnp.logical_not(early))
+            @pl.when(z + d >= RING)
             def _(d=d):
                 gather(d).start()
 
+    for there, later, device in neighbours:
+
+        @pl.when(there & jnp.logical_not(later))
+        def _(device=device):
+            pl.semaphore_signal(near, inc=1, device_id=device, device_id_type=MESH)
+
+    @pl.when(last)
+    def _():
+        pl.semaphore_signal(seam.at[0], inc=1, device_id=(lat, after), device_id_type=MESH)
+
+    @pl.when(last & has_up)
+    def _():
+        pl.semaphore_signal(seam.at[2], inc=1, device_id=(up, after), device_id_type=MESH)
+
+    @pl.when(last & has_down)
+    def _():
+        pl.semaphore_signal(seam.at[1], inc=1, device_id=(down, after), device_id_type=MESH)
+
+    load_x.wait()
+    pack(xp, lsend, rsend)
+    to_come = count(*[there & later for there, later, _ in neighbours])
+
+    @pl.when(to_come > 0)
+    def _():
+        pl.semaphore_wait(near, to_come)
+
     for c in own_across:
         c.start()
 
-    @pl.when(jnp.logical_not(early))
-    def _():
-        load_x.wait()
-        pack(xp, lsend, rsend)
-
-    to_right.start()
-
-    @pl.when(jnp.logical_not(first))
+    held_right = late & (g == PLANE - 1) & jnp.logical_not(last)
+    held_left = (late & (g == 0)) | last
+
+    @pl.when(jnp.logical_not(held_right))
+    def _():
+        to_right.start()
+
+    @pl.when(jnp.logical_not(first | held_left))
     def _():
         to_left.start()
 
@@ -352,14 +388,59 @@
         def _(copies=copies):
             copies[1].start()
 
-    @pl.when(jnp.logical_not(early))
-    def _():
-        prepare()
+    def step_out(n):
+        for side in range(2):
+            there = plane(2**n if side == 0 else PLANE - 2**n)
+            pl.semaphore_signal(known.at[n, side], inc=1, device_id=there, device_id_type=MESH)
+
+    def step_in(n):
+        for side in range(2):
+            pl.semaphore_wait(known.at[n, side], 1)
+
+    def answer():
+        for d in range(RING - 1, 0, -1):
+
+            @pl.when(z < d)
+            def _(d=d):
+                pl.semaphore_wait(hello.at[d], 1)
+                gather(RING - d).start()
+
+    @pl.when(is_polar)
+    def _():
+        step_out(0)
+
+    prepare_base()
+
+    @pl.when(is_polar)
+    def _():
+        step_in(0)
+        step_out(1)
+
+    prepare_band()
+
+    @pl.when(is_polar)
+    def _():
+        step_in(1)
+        step_out(2)
+
+    @pl.when(is_polar)
+    def _():
+        answer()
+        prepare_polar()
 
     for c, d in zip(own_across, passed_on):
         c.wait_recv()
         d.start()
 
+    for n, there, copy in ((0, first, to_left), (1, first & has_up, to_up[1]), (2, first & has_down, to_down[1])):
+
+        @pl.when(there)
+        def _(n=n, copy=copy):
+            pl.semaphore_wait(seam.at[n], 1)
+            copy.start()
+
+    pl.when(held_right)(to_right.start)
+    pl.when(held_left)(to_left.start)
     load_w.wait()
     for k in range(BASES):
         own_sibling[k].wait_recv()
@@ -377,15 +458,10 @@
 
     @pl.when(is_polar)
     def _():
-        load_z.wait()
-        for d in (4, 5, 3, 6, 2, 7, 1):
+        for d in range(1, RING):
             gather(d).wait_recv()
-
-            @pl.when(early & jnp.logical_not(early_at(RING - d)))
-            def _(d=d):
-                gather(RING - d).start()
-
         sources = split(xz[...].reshape(CH, CH))
+        step_in(2)
         for half in range(2):
             rows = slice(128 * half, 128 * half + 128)
             taps = [dot3((chi[k, rows], clo[k, rows]), sources) for k in range(BASES)]
@@ -394,11 +470,6 @@
                 partial(n).start()
 
     to_right.wait_recv()
-
-    @pl.when(first)
-    def _():
-        to_left.start()
-
     to_left.wait_recv()
     sub = iota((8, CH), 0)
 
@@ -406,11 +477,6 @@
     def _():
         for c in to_down:
             c.wait_recv()
-
-        @pl.when(first)
-        def _():
-            to_up[1].start()
-
         lrecv[0] = jnp.where(sub < 4, corner[0], lrecv[0])
         rrecv[0] = jnp.where(sub < 4, corner[1], rrecv[0])
 
@@ -422,11 +488,6 @@
     def _():
         for c in to_up:
             c.wait_recv()
-
-        @pl.when(first)
-        def _():
-            to_down[1].start()
-
         lrecv[GROUPS - 1] = jnp.where(sub < 4, lrecv[GROUPS - 1], corner[2])
         rrecv[GROUPS - 1] = jnp.where(sub < 4, rrecv[GROUPS - 1], corner[3])
 
@@ -534,6 +595,10 @@
             dma((RING,)),
             dma((PLANE,)),
             dma((PLANE,)),
+            pltpu.SemaphoreType.REGULAR((3, 2)),
+            pltpu.SemaphoreType.REGULAR((RING,)),
+            pltpu.SemaphoreType.REGULAR,
+            pltpu.SemaphoreType.REGULAR((3,)),
         ],
         compiler_params=pltpu.CompilerParams(
             collective_id=0, has_side_effects=True, vmem_limit_bytes=32 * 1024 * 1024

time: 29.2 us -> 27.6 us (0.945)
  the two profiles are of different devices: /device:TPU:8 before, /device:TPU:2 now
where the time goes in v3:
time: 27.6 us; the launch traced here: 27.5 us
  Pallas kernels  26.7 us (97%)
  local copies, waits for them, and re-layouts  0.8 us (3%)
    pallas_call x1, Pallas kernels, on_device(): pl.pallas_call(kernel, out_shape=pltpu.VMEM((ROWS, COLS, CH), F32), in_sp...  26.7 us
    unnamed x1, local copies, waits for them, and re-layouts  0.8 us

profile of v3, /device:TPU:2, one launch (start us, length us, event | category | flops | bytes accessed | tf_op | source)
XLA Modules:
  0.0 27.5 jit_solution(4858047995904397920)
XLA Ops:
  0.0 26.7 %disco.1 = f32[64,8,256]{2,1,0:T(8,128)S(1)} custom-call(f32[64,8,256]{2,1,0:T(8,128)} %atm.1, f32[5,5,3,64]{3,2,1,0:T(4,128)} %bitcast.2, f32[2,3,2,4,1024]{4,3,2,1,0:T(4,128)} %polar_in.1, s32[1,64]{1,0:T(1,128)} %bitcast.3, f32[1,3,64,256]{3,2,1,0:T(8,128)} %w_in.1, f32[1,256]{1,0:T(1,128)} %bias_in.1), custom_call_target="tpu_custom_call" | custom-call | tf_op jit(solution)/shard_map/disco/pallas_call | solution.py:557
  26.7 0.8 %copy.8 = f32[64,8,256]{2,1,0:T(8,128)} copy(f32[64,8,256]{2,1,0:T(8,128)S(1)} %disco.1) | data formatting | bytes 1048576

commit v4 on v3

--- a/solution.py
+++ b/solution.py
@@ -270,10 +270,7 @@
             def _(d=d):
                 greet(ring(d))
 
-        load_p.start()
-
-    for c in (load_x, load_d, load_wid, load_w, load_b):
-        c.start()
+    load_x.start()
 
     def prepare_base():
         load_d.wait()
@@ -321,19 +318,19 @@
 
     @pl.when(is_polar)
     def _():
+        load_z.wait()
+        for d in range(1, RING):
+
+            @pl.when(z + d >= RING)
+            def _(d=d):
+                gather(d).start()
+
         for d in range(1, RING):
 
             @pl.when(z + d >= RING)
             def _(d=d):
                 pl.semaphore_signal(hello.at[d], inc=1, device_id=ring(d), device_id_type=MESH)
 
-        load_z.wait()
-        for d in (4, 3, 5, 2, 6, 1, 7):
-
-            @pl.when(z + d >= RING)
-            def _(d=d):
-                gather(d).start()
-
     for there, later, device in neighbours:
 
         @pl.when(there & jnp.logical_not(later))
@@ -352,6 +349,10 @@
     def _():
         pl.semaphore_signal(seam.at[1], inc=1, device_id=(down, after), device_id_type=MESH)
 
+    for c in (load_w, load_d, load_wid, load_b):
+        c.start()
+
+    pl.when(is_polar)(load_p.start)
     load_x.wait()
     pack(xp, lsend, rsend)
     to_come = count(*[there & later for there, later, _ in neighbours])
@@ -425,8 +426,9 @@
 
     @pl.when(is_polar)
     def _():
-        answer()
+        pl.when(z >= RING // 4)(answer)
         prepare_polar()
+        pl.when(z < RING // 4)(answer)
 
     for c, d in zip(own_across, passed_on):
         c.wait_recv()

time: 27.6 us -> 27.1 us (0.982)
  the two profiles are of different devices: /device:TPU:2 before, /device:TPU:64 now
where the time goes in v4:
time: 27.1 us; the launch traced here: 27 us
  Pallas kernels  26.2 us (97%)
  local copies, waits for them, and re-layouts  0.8 us (3%)
    pallas_call x1, Pallas kernels, on_device(): pl.pallas_call(kernel, out_shape=pltpu.VMEM((ROWS, COLS, CH), F32), in_sp...  26.2 us
    unnamed x1, local copies, waits for them, and re-layouts  0.8 us

profile of v4, /device:TPU:64, one launch (start us, length us, event | category | flops | bytes accessed | tf_op | source)
XLA Modules:
  0.0 27.0 jit_solution(6277243616460338279)
XLA Ops:
  0.0 26.2 %disco.1 = f32[64,8,256]{2,1,0:T(8,128)S(1)} custom-call(f32[64,8,256]{2,1,0:T(8,128)} %atm.1, f32[5,5,3,64]{3,2,1,0:T(4,128)} %bitcast.2, f32[2,3,2,4,1024]{4,3,2,1,0:T(4,128)} %polar_in.1, s32[1,64]{1,0:T(1,128)} %bitcast.3, f32[1,3,64,256]{3,2,1,0:T(8,128)} %w_in.1, f32[1,256]{1,0:T(1,128)} %bias_in.1), custom_call_target="tpu_custom_call" | custom-call | tf_op jit(solution)/shard_map/disco/pallas_call | solution.py:559
  26.2 0.8 %copy.8 = f32[64,8,256]{2,1,0:T(8,128)} copy(f32[64,8,256]{2,1,0:T(8,128)S(1)} %disco.1) | data formatting | bytes 1048576

commit v5 on v4

--- a/solution.py
+++ b/solution.py
@@ -456,7 +456,11 @@
 
     def partial(n):
         d = distance(n)
-        return remote(mixp.at[pl.ds(16 * n, 16)], rs.at[n], rsem_s.at[n], rsem_r.at[n], plane(d))
+        return remote(mixp.at[pl.ds(16 * n, 16)], rs.at[n], rsem_s, rsem_r, plane(d))
+
+    def partials():
+        rows = rs.at[pl.ds(0, PLANE - 1)]
+        return remote(rows, rows, rsem_s, rsem_r, plane(1))
 
     @pl.when(is_polar)
     def _():
@@ -514,35 +518,34 @@
         mixed = mix(jnp.concatenate([tile[128 * k : 128 * k + 128] for k in range(BASES)], axis=1))
         out[TILE * s : TILE * s + TILE] = gelu(mixed + shift).reshape(TILE, COLS, CH)
 
+    for c in own_across + own_sibling + passed_on + [to_left, to_right]:
+        c.wait_send()
+
+    @pl.when(has_up)
+    def _():
+        for c in to_up:
+            c.wait_send()
+
+    @pl.when(has_down)
+    def _():
+        for c in to_down:
+            c.wait_send()
+
+    @pl.when(is_polar)
+    def _():
+        for d in range(1, RING):
+            gather(d).wait_send()
+        partials().wait_send()
+
     @pl.when(is_polar)
     def _():
         total = mixp[16 * PLANE - 16 : 16 * PLANE, :]
+        partials().wait_recv()
         for n in range(PLANE - 1):
-            partial(n).wait_recv()
             total = total + rs[n]
         total = gelu(total + shift)
         for p in range(2):
             out[p + south * (ROWS - 1 - 2 * p)] = total[8 * p : 8 * p + 8]
-
-    for c in own_across + own_sibling + passed_on + [to_left, to_right]:
-        c.wait_send()
-
-    @pl.when(has_up)
-    def _():
-        for c in to_up:
-            c.wait_send()
-
-    @pl.when(has_down)
-    def _():
-        for c in to_down:
-            c.wait_send()
-
-    @pl.when(is_polar)
-    def _():
-        for d in range(1, RING):
-            gather(d).wait_send()
-        for n in range(PLANE - 1):
-            partial(n).wait_send()
 
 
 def on_device(atmosphere, disc_basis, polar_basis, widths, weights, channel_bias):
@@ -595,8 +598,8 @@
             dma((BASES, 3)),
             dma((RING,)),
             dma((RING,)),
-            dma((PLANE,)),
-            dma((PLANE,)),
+            dma,
+            dma,
             pltpu.SemaphoreType.REGULAR((3, 2)),
             pltpu.SemaphoreType.REGULAR((RING,)),
             pltpu.SemaphoreType.REGULAR,

time: 27.1 us -> 26.8 us (0.989)
  Pallas kernels: 26.2 us -> 25.8 us
    pallas_call x1, Pallas kernels: 26.2 us -> 25.8 us  [on_device(): pl.pallas_call(kernel, out_shape=pltpu.VMEM((ROWS, COLS, CH), F32), in_sp...]
where the time goes in v5:
time: 26.8 us; the launch traced here: 26.6 us
  Pallas kernels  25.8 us (96%)
  local copies, waits for them, and re-layouts  0.8 us (3%)
    pallas_call x1, Pallas kernels, on_device(): pl.pallas_call(kernel, out_shape=pltpu.VMEM((ROWS, COLS, CH), F32), in_sp...  25.8 us
    unnamed x1, local copies, waits for them, and re-layouts  0.8 us

profile of v5, /device:TPU:64, one launch (start us, length us, event | category | flops | bytes accessed | tf_op | source)
XLA Modules:
  0.0 26.6 jit_solution(7390813103496243169)
XLA Ops:
  0.0 25.8 %disco.1 = f32[64,8,256]{2,1,0:T(8,128)S(1)} custom-call(f32[64,8,256]{2,1,0:T(8,128)} %atm.1, f32[5,5,3,64]{3,2,1,0:T(4,128)} %bitcast.2, f32[2,3,2,4,1024]{4,3,2,1,0:T(4,128)} %polar_in.1, s32[1,64]{1,0:T(1,128)} %bitcast.3, f32[1,3,64,256]{3,2,1,0:T(8,128)} %w_in.1, f32[1,256]{1,0:T(1,128)} %bias_in.1), custom_call_target="tpu_custom_call" | custom-call | tf_op jit(solution)/shard_map/disco/pallas_call | solution.py:562
  25.8 0.8 %copy.8 = f32[64,8,256]{2,1,0:T(8,128)} copy(f32[64,8,256]{2,1,0:T(8,128)S(1)} %disco.1) | data formatting | bytes 1048576

commit v6 on v5

--- a/solution.py
+++ b/solution.py
@@ -227,19 +227,19 @@
     late = z >= RING // 2
     turn = PLANE - 1 - 2 * g
     turning = is_polar & ((g == 0) | (g == PLANE - 1))
-    odd = lon % 2 == 1
-    whole = lon >= 0
-
+
+    even = lon % 2 == 0
+    above, below = lat == LAT - 1, lat != LAT - 2
     neighbours = [
-        (jnp.logical_not(last), whole, (lat, after)),
-        (jnp.logical_not(first), jnp.logical_not(whole), (lat, before)),
-        (has_up, jnp.logical_not(whole), (up, lon)),
-        (has_down, whole, (down, lon)),
-        (has_up & jnp.logical_not(last), whole, (up, after)),
-        (has_down & jnp.logical_not(last), whole, (down, after)),
-        (has_up & jnp.logical_not(first), jnp.logical_not(whole), (up, before)),
-        (has_down & jnp.logical_not(first), jnp.logical_not(whole), (down, before)),
-        (whole, jnp.logical_not(odd), across),
+        (jnp.logical_not(last), even, (lat, after)),
+        (jnp.logical_not(first), even, (lat, before)),
+        (has_up, above, (up, lon)),
+        (has_down, below, (down, lon)),
+        (has_up & jnp.logical_not(last), above | ((lat == 2) & even), (up, after)),
+        (has_down & jnp.logical_not(last), (lat == 0) | (below & even), (down, after)),
+        (has_up & jnp.logical_not(first), above | ((lat == 2) & even), (up, before)),
+        (has_down & jnp.logical_not(first), (lat == 0) | (below & even), (down, before)),
+        (lat >= 0, is_polar, across),
         (turning, g == 0, (lat, lon + turn)),
     ]
 

time: 26.8 us -> 26.4 us (0.985)
  Pallas kernels: 25.8 us -> 25.4 us
    pallas_call x1, Pallas kernels: 25.8 us -> 25.4 us  [on_device(): pl.pallas_call(kernel, out_shape=pltpu.VMEM((ROWS, COLS, CH), F32), in_sp...]
where the time goes in v6:
time: 26.4 us; the launch traced here: 26.2 us
  Pallas kernels  25.4 us (96%)
  local copies, waits for them, and re-layouts  0.8 us (3%)
    pallas_call x1, Pallas kernels, on_device(): pl.pallas_call(kernel, out_shape=pltpu.VMEM((ROWS, COLS, CH), F32), in_sp...  25.4 us
    unnamed x1, local copies, waits for them, and re-layouts  0.8 us

profile of v6, /device:TPU:64, one launch (start us, length us, event | category | flops | bytes accessed | tf_op | source)
XLA Modules:
  0.0 26.2 jit_solution(16568400186068652061)
XLA Ops:
  0.0 25.4 %disco.1 = f32[64,8,256]{2,1,0:T(8,128)S(1)} custom-call(f32[64,8,256]{2,1,0:T(8,128)} %atm.1, f32[5,5,3,64]{3,2,1,0:T(4,128)} %bitcast.2, f32[2,3,2,4,1024]{4,3,2,1,0:T(4,128)} %polar_in.1, s32[1,64]{1,0:T(1,128)} %bitcast.3, f32[1,3,64,256]{3,2,1,0:T(8,128)} %w_in.1, f32[1,256]{1,0:T(1,128)} %bias_in.1), custom_call_target="tpu_custom_call" | custom-call | tf_op jit(solution)/shard_map/disco/pallas_call | solution.py:562
  25.4 0.8 %copy.8 = f32[64,8,256]{2,1,0:T(8,128)} copy(f32[64,8,256]{2,1,0:T(8,128)S(1)} %disco.1) | data formatting | bytes 1048576

commit v7 on v6

--- a/solution.py
+++ b/solution.py
@@ -293,7 +293,7 @@
         pl.semaphore_wait(barrier, greeted)
 
     def gather(d):
-        return remote(xz.at[:, z], xz.at[:, z], zsem_s.at[d], zsem_r.at[d], ring(d))
+        return remote(xz.at[:, z], xz.at[:, z], zsem_s.at[d], zsem_r, ring(d))
 
     def shard(k, n, source_lat, device):
         rows = pl.ds(pl.multiple_of(64 * source_lat, 64), 64)
@@ -464,8 +464,8 @@
 
     @pl.when(is_polar)
     def _():
-        for d in range(1, RING):
-            gather(d).wait_recv()
+        rows = xz.at[:, pl.ds(0, RING - 1)]
+        remote(rows, rows, zsem_s.at[0], zsem_r, ring(1)).wait_recv()
         sources = split(xz[...].reshape(CH, CH))
         step_in(2)
         for half in range(2):
@@ -597,7 +597,7 @@
             dma((BASES, 3)),
             dma((BASES, 3)),
             dma((RING,)),
-            dma((RING,)),
+            dma,
             dma,
             dma,
             pltpu.SemaphoreType.REGULAR((3, 2)),

time: 26.4 us -> 26.3 us (level)
  no operation moved by 1% of the time
where the time goes in v7:
time: 26.3 us; the launch traced here: 26.1 us
  Pallas kernels  25.3 us (96%)
  local copies, waits for them, and re-layouts  0.8 us (3%)
    pallas_call x1, Pallas kernels, on_device(): pl.pallas_call(kernel, out_shape=pltpu.VMEM((ROWS, COLS, CH), F32), in_sp...  25.3 us
    unnamed x1, local copies, waits for them, and re-layouts  0.8 us

profile of v7, /device:TPU:64, one launch (start us, length us, event | category | flops | bytes accessed | tf_op | source)
XLA Modules:
  0.0 26.1 jit_solution(6924896818436761188)
XLA Ops:
  0.0 25.3 %disco.1 = f32[64,8,256]{2,1,0:T(8,128)S(1)} custom-call(f32[64,8,256]{2,1,0:T(8,128)} %atm.1, f32[5,5,3,64]{3,2,1,0:T(4,128)} %bitcast.2, f32[2,3,2,4,1024]{4,3,2,1,0:T(4,128)} %polar_in.1, s32[1,64]{1,0:T(1,128)} %bitcast.3, f32[1,3,64,256]{3,2,1,0:T(8,128)} %w_in.1, f32[1,256]{1,0:T(1,128)} %bias_in.1), custom_call_target="tpu_custom_call" | custom-call | tf_op jit(solution)/shard_map/disco/pallas_call | solution.py:562
  25.3 0.8 %copy.8 = f32[64,8,256]{2,1,0:T(8,128)} copy(f32[64,8,256]{2,1,0:T(8,128)S(1)} %disco.1) | data formatting | bytes 1048576

commit v8 on v7

--- a/solution.py
+++ b/solution.py
@@ -426,9 +426,9 @@
 
     @pl.when(is_polar)
     def _():
-        pl.when(z >= RING // 4)(answer)
+        pl.when(z >= RING // 2 - 1)(answer)
         prepare_polar()
-        pl.when(z < RING // 4)(answer)
+        pl.when(z < RING // 2 - 1)(answer)
 
     for c, d in zip(own_across, passed_on):
         c.wait_recv()

time: 26.3 us -> 26.3 us (level)
  no operation moved by 1% of the time
where the time goes in v8:
time: 26.3 us; the launch traced here: 26.1 us
  Pallas kernels  25.3 us (96%)
  local copies, waits for them, and re-layouts  0.8 us (3%)
    pallas_call x1, Pallas kernels, on_device(): pl.pallas_call(kernel, out_shape=pltpu.VMEM((ROWS, COLS, CH), F32), in_sp...  25.3 us
    unnamed x1, local copies, waits for them, and re-layouts  0.8 us

profile of v8, /device:TPU:64, one launch (start us, length us, event | category | flops | bytes accessed | tf_op | source)
XLA Modules:
  0.0 26.1 jit_solution(6335592882110703539)
XLA Ops:
  0.0 25.3 %disco.1 = f32[64,8,256]{2,1,0:T(8,128)S(1)} custom-call(f32[64,8,256]{2,1,0:T(8,128)} %atm.1, f32[5,5,3,64]{3,2,1,0:T(4,128)} %bitcast.2, f32[2,3,2,4,1024]{4,3,2,1,0:T(4,128)} %polar_in.1, s32[1,64]{1,0:T(1,128)} %bitcast.3, f32[1,3,64,256]{3,2,1,0:T(8,128)} %w_in.1, f32[1,256]{1,0:T(1,128)} %bias_in.1), custom_call_target="tpu_custom_call" | custom-call | tf_op jit(solution)/shard_map/disco/pallas_call | solution.py:562
  25.3 0.8 %copy.8 = f32[64,8,256]{2,1,0:T(8,128)} copy(f32[64,8,256]{2,1,0:T(8,128)S(1)} %disco.1) | data formatting | bytes 1048576
